TPU v7x, 32 devices: a whole 2x2x4 slice. The times are simulated.
32 devices in a mesh: parts: 2 (over y), req: 8 (over z, x), tensor: 2 (over core).
Axes of the slice: x: 2, y: 2, z: 4, core: 2. Of those that a mesh axis runs over, the one named last changes fastest.
Arguments:
- queries: bfloat16 [48, 64, 4096], P(('parts', 'req'), None, 'tensor'), parts along dimension 0, may hold values from -6 to 6
- block_keys: bfloat16 [48, 64, 512], P(('parts', 'req'), None, 'tensor'), parts along dimension 0, may hold values from -6 to 6
- block_values: bfloat16 [48, 64, 512], P(('parts', 'req'), None, 'tensor'), parts along dimension 0, may hold values from -6 to 6
- cache_keys: bfloat16 [48, 1024, 512], P(('parts', 'req'), None, 'tensor'), parts along dimension 0, may hold values from -6 to 6
- cache_values: bfloat16 [48, 1024, 512], P(('parts', 'req'), None, 'tensor'), parts along dimension 0, may hold values from -6 to 6
- block_len: int32 [16, 3], P(('parts', 'req')), parts along dimension 0, may hold values from 1 to 64, as said below
- prefix_len: int32 [16, 3], P(('parts', 'req')), parts along dimension 0, may hold values from 1 to 1024, as said below
- deferred: int32 [16, 3], P(('parts', 'req')), parts along dimension 0, may hold values 0 or 1
- route: int32 [16, 3], P(('parts', 'req')), parts along dimension 0, may hold values from 0 to 2, each once within a row
Outputs:
- attended: bfloat16 [48, 64, 4096], P(('parts', 'req'), None, 'tensor'), parts along dimension 0
There are 2 independent parts, one for each index of `parts`. A program takes and returns all parts, laid end to end along the dimension named above; each array names one. Nothing has to cross between parts.
Inputs may be any that keep to these rules, and one draw needn't show every extreme that they name: `block_len`: live tokens of a prompt block; some block has all 64. `prefix_len`: live tokens of a cached prefix; some prefix has all 1024. `route`: each device's row holds every partner number once.
All inputs are finite; a program needn't handle non-finite values. No bound on the sum of `deferred` on one device may be relied on, other than what follows from the above.
Results may differ from a plain program's by a relative error of at most 0.0028.
Values may be sent and summed in bfloat16 or wider, within the bound.
A program may use at most 64 MiB of HBM per device.

v0:
```python
import jax
import jax.numpy as jnp
from jax import lax
from jax.sharding import PartitionSpec as P

HEAD_DIM = 128


def from_behind(value, axis, by):
    peers = lax.axis_size(axis)
    return lax.ppermute(value, axis, [(i, (i + by) % peers) for i in range(peers)])


def attend_local(query, block_key, block_value, cache_key, cache_value, cache_valid, row_valid):
    rows = query.shape[0]
    groups = block_key.shape[1] // HEAD_DIM
    ratio = query.shape[1] // HEAD_DIM // groups
    query_four = query.reshape(rows, groups, ratio, HEAD_DIM)
    keys_all = jnp.concatenate([cache_key, block_key], axis=0).reshape(-1, groups, HEAD_DIM)
    values_all = jnp.concatenate([cache_value, block_value], axis=0).reshape(-1, groups, HEAD_DIM)
    scores = jnp.einsum(
        "igrd,jgd->grij", query_four, keys_all, preferred_element_type=jnp.float32
    ) / jnp.sqrt(jnp.float32(HEAD_DIM))
    position = jnp.arange(rows, dtype=jnp.int32)
    inner = (position[None, :] <= position[:, None]) & row_valid[None, :]
    outer = jnp.broadcast_to(cache_valid[None, :], (rows, cache_valid.shape[0]))
    visible = jnp.concatenate([outer, inner], axis=1)
    highest = jnp.max(jnp.where(visible, scores, jnp.float32(-1e30)), axis=-1, keepdims=True)
    weights = jnp.where(visible, jnp.exp(scores - highest), jnp.float32(0.0))
    totals = jnp.sum(weights, axis=-1)
    mixed = jnp.einsum(
        "grij,jgd->igrd",
        weights.astype(jnp.bfloat16),
        values_all,
        preferred_element_type=jnp.float32,
    )
    mixed = mixed / jnp.transpose(totals, (2, 0, 1))[..., None]
    mixed = mixed.reshape(rows, -1)
    return jnp.where(row_valid[:, None], mixed, jnp.float32(0.0)).astype(jnp.bfloat16)


def per_device(
    queries,
    block_keys,
    block_values,
    cache_keys,
    cache_values,
    block_len,
    prefix_len,
    deferred,
    route,
):
    req_count = lax.axis_size("req")
    distances = [1, req_count // 4, req_count // 2]
    hops = route.shape[1]
    rows = queries.shape[1]
    cache_rows = cache_keys.shape[1]
    row_valid_all = jnp.arange(rows, dtype=jnp.int32)[None, :] < block_len[0][:, None]
    cache_own_valid = jnp.arange(cache_rows, dtype=jnp.int32)[None, :] < prefix_len[0][:, None]
    deferred_flag = deferred[0] == 1
    fetched_keys = []
    fetched_values = []
    fetched_valid = []
    for offset_index in range(hops):
        got_key, got_value, got_valid = from_behind(
            (
                cache_keys[offset_index],
                cache_values[offset_index],
                cache_own_valid[offset_index].astype(jnp.bfloat16),
            ),
            "req",
            -distances[offset_index],
        )
        fetched_keys.append(got_key)
        fetched_values.append(got_value)
        fetched_valid.append(got_valid)
    stacked_keys = jnp.stack(fetched_keys)
    stacked_values = jnp.stack(fetched_values)
    stacked_valid = jnp.stack(fetched_valid)
    answers = []
    for block_index in range(hops):
        partner = route[0, block_index]
        cache_key = lax.dynamic_index_in_dim(stacked_keys, partner, 0, keepdims=False)
        cache_value = lax.dynamic_index_in_dim(stacked_values, partner, 0, keepdims=False)
        cache_valid = (
            lax.dynamic_index_in_dim(stacked_valid, partner, 0, keepdims=False) > 0.5
        ) & deferred_flag[block_index]
        answers.append(
            attend_local(
                queries[block_index],
                block_keys[block_index],
                block_values[block_index],
                cache_key,
                cache_value,
                cache_valid,
                row_valid_all[block_index],
            )
        )
    return jnp.stack(answers)


def solution(mesh):
    return jax.shard_map(
        per_device,
        mesh=mesh,
        in_specs=(
            P(("parts", "req"), None, "tensor"),
            P(("parts", "req"), None, "tensor"),
            P(("parts", "req"), None, "tensor"),
            P(("parts", "req"), None, "tensor"),
            P(("parts", "req"), None, "tensor"),
            P(("parts", "req"), None),
            P(("parts", "req"), None),
            P(("parts", "req"), None),
            P(("parts", "req"), None),
        ),
        out_specs=P(("parts", "req"), None, "tensor"),
        check_vma=False,
    )
```

profile of v0, /device:TPU:29, one launch (start us, length us, event | category | flops | bytes accessed | tf_op | source)
XLA Modules:
  0.0 114.9 jit_solution(5619183644599170903)
XLA Ops:
  0.0 1.5 %fusion.78 = (bf16[1,1024,256]{2,1,0:T(8,128)(2,1)S(1)}, bf16[1,1024,256]{2,1,0:T(8,128)(2,1)S(1)}, bf16[1,1024,256]{2,1,0:T(8,128)(2,1)S(1)}) fusion(bf16[3,1024,256]{2,1,0:T(8,128)(2,1)} %param.13), kind=kLoop, calls=%fused_computation.107 | loop fusion | bytes 3145728 | tf_op jit(solution)/shard_map/slice | solution.py:68
  1.5 1.0 copy.40
  2.5 1.1 collective-permute-start
  3.6 1.0 copy.41
  5.9 3.2 %collective-permute-start.5 = (bf16[1024]{0:T(1024)(128)(2,1)}, bf16[1024]{0:T(1024)(128)(2,1)}, u32[]{:S(2)}, u32[]{:S(2)}) collective-permute-start(bf16[1024]{0:T(1024)(128)(2,1)} %get-tuple-element.9), channel_id=1, source_target_pairs={{0,8},{2,10},{4,12},{6,14},{8,0},{10,2},{12,4},{14,6},{1,9},{3,11}... | collective-permute-start | bytes 6152 | tf_op jit(solution)/shard_map/ppermute | solution.py:11
  10.9 1.5 %fusion.79 = (bf16[1,1024,256]{2,1,0:T(8,128)(2,1)S(1)}, bf16[1,1024,256]{2,1,0:T(8,128)(2,1)S(1)}, bf16[1,1024,256]{2,1,0:T(8,128)(2,1)S(1)}) fusion(bf16[3,1024,256]{2,1,0:T(8,128)(2,1)} %param.12), kind=kLoop, calls=%fused_computation.108 | loop fusion | bytes 3145728 | tf_op jit(solution)/shard_map/slice | solution.py:67
  12.4 1.2 %slice_bitcast_fusion.2 = (bf16[8,8,16,128]{3,1,2,0:T(8,128)(2,1)S(1)}, bf16[8,8,16,128]{3,1,2,0:T(8,128)(2,1)S(1)}, bf16[8,8,16,128]{3,1,2,0:T(8,128)(2,1)S(1)}) fusion(bf16[3,64,2048]{2,1,0:T(8,128)(2,1)} %param.9), kind=kLoop, calls=%fused_computation.71 | loop fusion | bytes 1572864
  17.7 1.0 copy.42
  18.7 1.0 copy.43
  26.5 3.2 %collective-permute-done.4 = bf16[1024]{0:T(1024)(128)(2,1)} collective-permute-done((bf16[1024]{0:T(1024)(128)(2,1)}, bf16[1024]{0:T(1024)(128)(2,1)}, u32[]{:S(2)}, u32[]{:S(2)}) %collective-permute-start.4) | collective-permute-done | bytes 2080 | tf_op jit(solution)/shard_map/ppermute | solution.py:11
  30.3 4.0 %collective-permute-start.7 = (bf16[1024,256]{0,1:T(8,128)(2,1)S(1)}, bf16[1024,256]{0,1:T(8,128)(2,1)S(1)}, u32[]{:S(2)}, u32[]{:S(2)}) collective-permute-start(bf16[1024,256]{0,1:T(8,128)(2,1)S(1)} %bitcast.141), channel_id=1, source_target_pairs={{0,12},{2,14},{4,0},{6,2},{8,4},{10,6},{12,8},{14,10},{1,13},{3,15... | collective-permute-start | bytes 1572872 | tf_op jit(solution)/shard_map/ppermute | solution.py:11
  35.0 1.9 %and_reduce_fusion.2 = (pred[1024]{0:T(1024)(128)(4,1)S(1)}, pred[1024]{0:T(1024)(128)(4,1)S(1)}, pred[1024]{0:T(1024)(128)(4,1)S(1)}) fusion(pred[]{:T(512)} %bitcast.13, bf16[3,1024]{1,0:T(4,128)(2,1)S(1)} %pad_maximum_fusion.3, s32[]{:T(128)S(6)} %select_n.67, pred[]{:T(512)} %bitcast.43, s32[]{:T(128)S(6)} %select_n.75, pred[]{:T(512)} %bitcast.31, ...), kind=kLoop, calls=%fused_computation.82 | loop fusion | flops 10240 | bytes 9231 | tf_op jit(solution)/shard_map/and | solution.py:85
  37.5 1.3 %pad_add_fusion.1 = pred[64,1088]{1,0:T(8,128)(4,1)} fusion(pred[64,64]{1,0:T(8,128)(4,1)} %get-tuple-element.51, pred[1088]{0:T(1024)(128)(4,1)S(1)} %pad.11.clone), kind=kLoop, calls=%fused_computation.64 | loop fusion | flops 69632 | bytes 74816 | tf_op jit(solution)/shard_map/concatenate | solution.py:27
  38.9 1.0 collective-permute-start.8
  40.5 46.4 %collective-permute-done.2 = bf16[1024,256]{0,1:T(8,128)(2,1)S(1)} collective-permute-done((bf16[1024,256]{0,1:T(8,128)(2,1)}, bf16[1024,256]{0,1:T(8,128)(2,1)S(1)}, u32[]{:S(2)}, u32[]{:S(2)}) %collective-permute-start.2) | collective-permute-done | bytes 524320 | tf_op jit(solution)/shard_map/ppermute | solution.py:11
  86.9 1.4 %pad_maximum_fusion = bf16[3,1024,256]{1,2,0:T(8,128)(2,1)S(1)} fusion(bf16[1,1024,256]{1,2,0:T(8,128)(2,1)S(1)} %bitcast.145, bf16[1,1024,256]{1,2,0:T(8,128)(2,1)} %bitcast.5, bf16[1,1024,256]{1,2,0:T(8,128)(2,1)} %bitcast.3), kind=kLoop, calls=%fused_computation.33 | loop fusion | flops 1572864 | bytes 3145728 | tf_op jit(solution)/shard_map/stack | solution.py:78
  88.3 9.8 %collective-permute-done.8 = bf16[1024,256]{0,1:T(8,128)(2,1)S(1)} collective-permute-done((bf16[1024,256]{0,1:T(8,128)(2,1)S(1)}, bf16[1024,256]{0,1:T(8,128)(2,1)S(1)}, u32[]{:S(2)}, u32[]{:S(2)}) %collective-permute-start.8) | collective-permute-done | bytes 524320 | tf_op jit(solution)/shard_map/ppermute | solution.py:11
  98.6 1.0 copy.18
  99.9 1.9 %convolution_multiply_fusion.2 = f32[2,1088,64,8]{1,2,3,0:T(8,128)S(1)} fusion(bf16[64,2,128]{2,0,1:T(8,128)(2,1)S(1)} %copy.19, bf16[1024,2,128]{2,0,1:T(8,128)(2,1)} %copy.18, bf16[64,2,8,128]{3,2,1,0:T(8,128)(2,1)} %bitcast.139), kind=kOutput, calls=%fused_computation.14 | convolution fusion | flops 287440896 | bytes 5275648 | tf_op jit(solution)/shard_map/igrd,jgd->grij/dot_general | solution.py:21
  101.9 1.8 %fusion.86 = (f32[2,8,64]{2,1,0:T(8,128)S(1)}, bf16[2,8,64,1088]{3,2,1,0:T(8,128)(2,1)S(1)}) fusion(f32[2,1088,64,8]{1,2,3,0:T(8,128)S(1)} %convolution_multiply_fusion.2, pred[64,1088]{1,0:T(8,128)(4,1)S(1)} %copy-done.6), kind=kOutput, calls=%fused_computation.115 | output fusion | flops 5571647 | bytes 6758400 | tf_op jit(solution)/shard_map/sub | solution.py:29
  105.5 0.8 convolution_multiply_fusion.1
  106.4 1.8 %fusion.85 = (f32[2,8,64]{2,1,0:T(8,128)S(1)}, bf16[2,8,64,1088]{3,2,1,0:T(8,128)(2,1)S(1)}) fusion(f32[2,1088,64,8]{1,2,3,0:T(8,128)S(1)} %convolution_multiply_fusion.1, pred[64,1088]{1,0:T(8,128)(4,1)S(1)} %copy-done.5), kind=kOutput, calls=%fused_computation.114 | output fusion | flops 5571647 | bytes 6758400 | tf_op jit(solution)/shard_map/sub | solution.py:29
  110.9 1.8 %fusion.84 = (f32[2,8,64]{2,1,0:T(8,128)S(1)}, bf16[2,8,64,1088]{3,2,1,0:T(8,128)(2,1)S(1)}) fusion(f32[2,1088,64,8]{1,2,3,0:T(8,128)S(1)} %convolution_multiply_fusion, pred[64,1088]{1,0:T(8,128)(4,1)S(1)} %copy-done.4), kind=kOutput, calls=%fused_computation.113 | output fusion | flops 5571647 | bytes 6758400 | tf_op jit(solution)/shard_map/sub | solution.py:29
  113.9 1.0 pad_maximum_fusion.2
  (106 shorter events, 17.2 us)
Async XLA Ops:
  0.0 4.8 %copy-start.16 = (s32[1,3]{1,0:T(1,128)S(1)}, s32[1,3]{1,0:T(1,128)}, u32[]{:S(2)}) copy-start(s32[1,3]{1,0:T(1,128)} %param.15) | copy-start | bytes 40
  0.0 9.1 %copy-start.15 = (s32[1,3]{1,0:T(1,128)S(1)}, s32[1,3]{1,0:T(1,128)}, u32[]{:S(2)}) copy-start(s32[1,3]{1,0:T(1,128)} %param.17) | copy-start | bytes 40
  2.5 36.4 %collective-permute-start = (bf16[1024,256]{0,1:T(8,128)(2,1)}, bf16[1024,256]{0,1:T(8,128)(2,1)}, u32[]{:S(2)}, u32[]{:S(2)}) collective-permute-start(bf16[1024,256]{0,1:T(8,128)(2,1)} %bitcast.2), channel_id=1, source_target_pairs={{0,14},{2,0},{4,2},{6,4},{8,6},{10,8},{12,10},{14,12},{1,15},{3,1}... | collective-permute-start | bytes 1572872 | tf_op jit(solution)/shard_map/ppermute | solution.py:11
  4.6 35.9 %collective-permute-start.1 = (bf16[1024,256]{0,1:T(8,128)(2,1)}, bf16[1024,256]{0,1:T(8,128)(2,1)}, u32[]{:S(2)}, u32[]{:S(2)}) collective-permute-start(bf16[1024,256]{0,1:T(8,128)(2,1)} %bitcast.4), channel_id=1, source_target_pairs={{0,12},{2,14},{4,0},{6,2},{8,4},{10,6},{12,8},{14,10},{1,13},{3,15... | collective-permute-start | bytes 1572872 | tf_op jit(solution)/shard_map/ppermute | solution.py:11
  5.5 20.3 %collective-permute-start.3 = (bf16[1024]{0:T(1024)(128)(2,1)}, bf16[1024]{0:T(1024)(128)(2,1)}, u32[]{:S(2)}, u32[]{:S(2)}) collective-permute-start(bf16[1024]{0:T(1024)(128)(2,1)} %get-tuple-element.8), channel_id=1, source_target_pairs={{0,14},{2,0},{4,2},{6,4},{8,6},{10,8},{12,10},{14,12},{1,15},{3,1}... | collective-permute-start | bytes 6152 | tf_op jit(solution)/shard_map/ppermute | solution.py:11
  5.7 23.9 %collective-permute-start.4 = (bf16[1024]{0:T(1024)(128)(2,1)}, bf16[1024]{0:T(1024)(128)(2,1)}, u32[]{:S(2)}, u32[]{:S(2)}) collective-permute-start(bf16[1024]{0:T(1024)(128)(2,1)} %get-tuple-element.10), channel_id=1, source_target_pairs={{0,12},{2,14},{4,0},{6,2},{8,4},{10,6},{12,8},{14,10},{1,13},{3,15... | collective-permute-start | bytes 6152 | tf_op jit(solution)/shard_map/ppermute | solution.py:11
  5.9 24.4 %collective-permute-start.5 = (bf16[1024]{0:T(1024)(128)(2,1)}, bf16[1024]{0:T(1024)(128)(2,1)}, u32[]{:S(2)}, u32[]{:S(2)}) collective-permute-start(bf16[1024]{0:T(1024)(128)(2,1)} %get-tuple-element.9), channel_id=1, source_target_pairs={{0,8},{2,10},{4,12},{6,14},{8,0},{10,2},{12,4},{14,6},{1,9},{3,11}... | collective-permute-start | bytes 6152 | tf_op jit(solution)/shard_map/ppermute | solution.py:11
  10.9 2.7 %copy-start.2 = (bf16[3,64,256]{2,1,0:T(8,128)(2,1)S(1)}, bf16[3,64,256]{2,1,0:T(8,128)(2,1)}, u32[]{:S(2)}) copy-start(bf16[3,64,256]{2,1,0:T(8,128)(2,1)} %param.10) | copy-start | bytes 294916
  10.9 2.8 %copy-start.17 = (s32[1,3]{1,0:T(1,128)S(1)}, s32[1,3]{1,0:T(1,128)}, u32[]{:S(2)}) copy-start(s32[1,3]{1,0:T(1,128)} %param.16) | copy-start | bytes 40
  10.9 3.4 %copy-start.18 = (s32[1,3]{1,0:T(1,128)S(1)}, s32[1,3]{1,0:T(1,128)}, u32[]{:S(2)}) copy-start(s32[1,3]{1,0:T(1,128)} %param.14) | copy-start | bytes 40
  10.9 3.5 %copy-start.3 = (bf16[3,64,256]{2,1,0:T(8,128)(2,1)S(1)}, bf16[3,64,256]{2,1,0:T(8,128)(2,1)}, u32[]{:S(2)}) copy-start(bf16[3,64,256]{2,1,0:T(8,128)(2,1)} %param.11) | copy-start | bytes 294916
  14.4 6.5 %copy-start.9 = (pred[64]{0:T(512)(128)(4,1)}, pred[64]{0:T(512)(128)(4,1)S(1)}, u32[]{:S(2)}) copy-start(pred[64]{0:T(512)(128)(4,1)S(1)} %get-tuple-element.33) | copy-start | bytes 196
  14.4 6.5 %copy-start.11 = (pred[64]{0:T(512)(128)(4,1)}, pred[64]{0:T(512)(128)(4,1)S(1)}, u32[]{:S(2)}) copy-start(pred[64]{0:T(512)(128)(4,1)S(1)} %get-tuple-element.34) | copy-start | bytes 196
  14.4 6.5 %copy-start.13 = (pred[64]{0:T(512)(128)(4,1)}, pred[64]{0:T(512)(128)(4,1)S(1)}, u32[]{:S(2)}) copy-start(pred[64]{0:T(512)(128)(4,1)S(1)} %get-tuple-element.32) | copy-start | bytes 196
  19.9 9.7 %copy-start.1 = (bf16[1,1024,256]{1,2,0:T(8,128)(2,1)S(1)}, bf16[1,1024,256]{1,2,0:T(8,128)(2,1)}, u32[]{:S(2)}) copy-start(bf16[1,1024,256]{1,2,0:T(8,128)(2,1)} %copy.43) | copy-start | bytes 1572868
  25.7 61.2 %collective-permute-start.2 = (bf16[1024,256]{0,1:T(8,128)(2,1)}, bf16[1024,256]{0,1:T(8,128)(2,1)S(1)}, u32[]{:S(2)}, u32[]{:S(2)}) collective-permute-start(bf16[1024,256]{0,1:T(8,128)(2,1)} %bitcast.143), channel_id=1, source_target_pairs={{0,8},{2,10},{4,12},{6,14},{8,0},{10,2},{12,4},{14,6},{1,9},{3,11}... | collective-permute-start | bytes 1572872 | tf_op jit(solution)/shard_map/ppermute | solution.py:11
  29.7 58.6 %collective-permute-start.6 = (bf16[1024,256]{0,1:T(8,128)(2,1)S(1)}, bf16[1024,256]{0,1:T(8,128)(2,1)S(1)}, u32[]{:S(2)}, u32[]{:S(2)}) collective-permute-start(bf16[1024,256]{0,1:T(8,128)(2,1)S(1)} %bitcast.142), channel_id=1, source_target_pairs={{0,14},{2,0},{4,2},{6,4},{8,6},{10,8},{12,10},{14,12},{1,15},{3,1}... | collective-permute-start | bytes 1572872 | tf_op jit(solution)/shard_map/ppermute | solution.py:11
  30.3 58.0 %collective-permute-start.7 = (bf16[1024,256]{0,1:T(8,128)(2,1)S(1)}, bf16[1024,256]{0,1:T(8,128)(2,1)S(1)}, u32[]{:S(2)}, u32[]{:S(2)}) collective-permute-start(bf16[1024,256]{0,1:T(8,128)(2,1)S(1)} %bitcast.141), channel_id=1, source_target_pairs={{0,12},{2,14},{4,0},{6,2},{8,4},{10,6},{12,8},{14,10},{1,13},{3,15... | collective-permute-start | bytes 1572872 | tf_op jit(solution)/shard_map/ppermute | solution.py:11
  38.9 59.3 %collective-permute-start.8 = (bf16[1024,256]{0,1:T(8,128)(2,1)S(1)}, bf16[1024,256]{0,1:T(8,128)(2,1)S(1)}, u32[]{:S(2)}, u32[]{:S(2)}) collective-permute-start(bf16[1024,256]{0,1:T(8,128)(2,1)S(1)} %bitcast.140), channel_id=1, source_target_pairs={{0,8},{2,10},{4,12},{6,14},{8,0},{10,2},{12,4},{14,6},{1,9},{3,11}... | collective-permute-start | bytes 1572872 | tf_op jit(solution)/shard_map/ppermute | solution.py:11
  99.9 1.9 %copy-start.6 = (pred[64,1088]{1,0:T(8,128)(4,1)S(1)}, pred[64,1088]{1,0:T(8,128)(4,1)}, u32[]{:S(2)}) copy-start(pred[64,1088]{1,0:T(8,128)(4,1)} %pad_add_fusion) | copy-start | bytes 208900
  101.9 1.9 %copy-start.8 = (bf16[64,2,128]{2,0,1:T(8,128)(2,1)S(1)}, bf16[64,2,128]{2,0,1:T(8,128)(2,1)}, u32[]{:S(2)}) copy-start(bf16[64,2,128]{2,0,1:T(8,128)(2,1)} %copy.14) | copy-start | bytes 98308
  103.7 1.1 copy-start.14
  106.4 1.8 %copy-start.7 = (bf16[64,2,128]{2,0,1:T(8,128)(2,1)S(1)}, bf16[64,2,128]{2,0,1:T(8,128)(2,1)}, u32[]{:S(2)}) copy-start(bf16[64,2,128]{2,0,1:T(8,128)(2,1)} %copy.23) | copy-start | bytes 98308
  108.2 1.1 copy-start.12
  (4 other events, 3.9 us)
where the time goes:
time: 117 us; the launch traced here: 115 us
  waiting for transfers between devices  60.2 us (51%)
  local copies, waits for them, and re-layouts  18.7 us (16%)
  other arithmetic  14.3 us (12%)
  starting transfers between devices  9.9 us (8%)
  between operations  6.06 us (5%)
  matrix products  5.76 us (5%)
    ppermute x9, waiting for transfers between devices, from_behind(): lax.ppermute(value, axis, [(i, (i + by) % peers) for i in range(peers)])  60.2 us
    ppermute x9, starting transfers between devices, from_behind(): lax.ppermute(value, axis, [(i, (i + by) % peers) for i in range(peers)])  9.9 us
    unnamed x48, local copies, waits for them, and re-layouts  7.42 us
    sub x3, other arithmetic, attend_local(): weights = jnp.where(visible, jnp.exp(scores - highest), jnp.float32(0.0))  5.51 us
    dot_general x3, matrix products, attend_local(): jnp.einsum('igrd,jgd->grij', query_four, keys_all, preferred_element_type...  3.48 us
    concatenate x3, other arithmetic, attend_local(): visible = jnp.concatenate([outer, inner], axis=1)  2.65 us
  transfers between devices with their start and end apart: 9, of which 4 were waited for; matrix products, arithmetic and copies ran while one was open for 17% of the time, Pallas kernels for 0%

commit v1 on v0

v1 whole, which is shorter than its diff:
```python
import functools
import math

import jax
import jax.numpy as jnp
from jax import lax
from jax.experimental import pallas as pl
from jax.experimental.pallas import tpu as pltpu
from jax.sharding import PartitionSpec as P

HEAD_DIM = 128
LANES = 128
HIDDEN = -1e30
LEVELS = 32767.0
MESH = pl.DeviceIdType.MESH
SCALE = math.log2(math.e) / math.sqrt(HEAD_DIM)


def dot_nt(a, b):
    return lax.dot_general(a, b, (((1,), (1,)), ((), ())), preferred_element_type=jnp.float32)


def heads_to_lanes(column, rows, ratio, first, into):
    lane = lax.broadcasted_iota(jnp.int32, (rows, LANES), 1)
    for h in range(ratio):
        piece = jnp.broadcast_to(column[h * rows : (h + 1) * rows, :], (rows, LANES))
        into = jnp.where(lane == first + h, piece, into)
    return into


def lanes_to_heads(packed, ratio, first):
    return jnp.concatenate([packed[:, first + h : first + h + 1] for h in range(ratio)], axis=0)


def kernel(
    distances,
    ratio,
    route_ref,
    block_len_ref,
    prefix_len_ref,
    deferred_ref,
    q_ref,
    bk_ref,
    bv_ref,
    ck_hbm,
    cv_hbm,
    out_ref,
    ck,
    cv,
    q_out,
    q_in,
    top_out,
    top_in,
    sum_out,
    sum_in,
    stat_out,
    stat_in,
    inner,
    mixed,
    cache_sem,
    q_sem,
    top_sem,
    sum_sem,
    stat_sem,
):
    peers = lax.axis_size("req")
    me = lax.axis_index("req")
    hops, rows = q_ref.shape[0], q_ref.shape[1]
    groups = bk_ref.shape[2] // HEAD_DIM
    cache_rows = ck.shape[1]
    stacked = ratio * rows
    order = list(reversed(range(hops)))
    holder = [lax.rem(me + distances[k], peers) for k in range(hops)]
    asker = [lax.rem(me + peers - distances[k], peers) for k in range(hops)]

    barrier = pltpu.get_barrier_semaphore()
    for k in range(hops):
        for peer in (holder[k], asker[k]):
            pl.semaphore_signal(barrier, inc=1, device_id={"req": peer}, device_id_type=MESH)

    loads = {}
    for k in order:
        loads[k] = [
            pltpu.make_async_copy(ck_hbm.at[k], ck.at[k], cache_sem.at[k, 0]),
            pltpu.make_async_copy(cv_hbm.at[k], cv.at[k], cache_sem.at[k, 1]),
        ]
        for load in loads[k]:
            load.start()

    block_of = []
    for k in range(hops):
        block = jnp.int32(0)
        for c in range(1, hops):
            block = jnp.where(route_ref[0, c] == k, jnp.int32(c), block)
        block_of.append(block)

    def send(source, target, sems, where, peer):
        return pltpu.make_async_remote_copy(
            src_ref=source.at[where],
            dst_ref=target.at[where],
            send_sem=sems.at[(0, *where)],
            recv_sem=sems.at[(1, *where)],
            device_id={"req": peer},
            device_id_type=MESH,
        )

    for k in order:
        for g in range(groups):
            for h in range(ratio):
                at = (g * ratio + h) * HEAD_DIM
                q_out[k, g, h * rows : (h + 1) * rows, :] = q_ref[block_of[k], :, at : at + HEAD_DIM]

    pl.semaphore_wait(barrier, 2 * hops)

    asks, tops, sums, stats = {}, {}, {}, {}
    for k in order:
        for g in range(groups):
            asks[k, g] = send(q_out, q_in, q_sem, (k, g), holder[k])
            asks[k, g].start()

    row = lax.rem(lax.broadcasted_iota(jnp.int32, (stacked, rows), 0), rows)
    column = lax.broadcasted_iota(jnp.int32, (stacked, rows), 1)
    for k in order:
        visible = (column <= row) & (column < block_len_ref[0, block_of[k]])
        packed = jnp.zeros((rows, LANES), jnp.float32)
        for g in range(groups):
            cols = slice(g * HEAD_DIM, (g + 1) * HEAD_DIM)
            scores = dot_nt(q_out[k, g], bk_ref[block_of[k], :, cols]) * SCALE
            scores = jnp.where(visible, scores, HIDDEN)
            inner[k, g] = scores
            packed = heads_to_lanes(
                jnp.max(scores, axis=1, keepdims=True), rows, ratio, g * ratio, packed
            )
        whole = jnp.concatenate([packed, jnp.zeros((LANES - rows, LANES), jnp.float32)], axis=0)
        top_out[k] = whole.T[: groups * ratio, :]
        tops[k] = send(top_out, top_in, top_sem, (k,), holder[k])
        tops[k].start()

    place = lax.broadcasted_iota(jnp.int32, (1, cache_rows), 1)
    pad = jnp.zeros((LANES - groups * ratio, LANES), jnp.float32)
    for k in order:
        bias = jnp.where(place < prefix_len_ref[0, k], 0.0, HIDDEN)
        for load in loads[k]:
            load.wait()
        tops[k].wait_recv()
        asked_top = jnp.concatenate([top_in[k], pad], axis=0).T[:rows, :]
        for g in range(groups):
            cols = slice(g * HEAD_DIM, (g + 1) * HEAD_DIM)
            asks[k, g].wait_recv()
            scores = dot_nt(q_in[k, g], ck[k, :, cols]) * SCALE + bias
            top = jnp.maximum(
                lanes_to_heads(asked_top, ratio, g * ratio), jnp.max(scores, axis=1, keepdims=True)
            )
            weights = jnp.exp2(scores - top)
            total = jnp.sum(weights, axis=1, keepdims=True)
            part = jnp.dot(
                weights.astype(jnp.bfloat16), cv[k, :, cols], preferred_element_type=jnp.float32
            )
            largest = jnp.maximum(jnp.max(jnp.abs(part), axis=1, keepdims=True), 1e-33)
            coded = jnp.round(part * (LEVELS / largest))
            sum_out[k, g] = coded.astype(jnp.int32).astype(jnp.int16)
            sums[k, g] = send(sum_out, sum_in, sum_sem, (k, g), asker[k])
            sums[k, g].start()
            zeros = jnp.zeros((rows, LANES), jnp.float32)
            upper = heads_to_lanes(top, rows, ratio, 0, zeros)
            upper = heads_to_lanes(largest, rows, ratio, ratio, upper)
            lower = heads_to_lanes(total, rows, ratio, 0, zeros)
            stat_out[k, g] = jnp.concatenate([upper, lower], axis=0).T[: 2 * ratio, :]
            stats[k, g] = send(stat_out, stat_in, stat_sem, (k, g), asker[k])
            stats[k, g].start()

    pad = jnp.zeros((LANES - 2 * ratio, LANES), jnp.float32)
    for k in order:
        continues = deferred_ref[0, block_of[k]] == 1
        live = row[:, :1] < block_len_ref[0, block_of[k]]
        for g in range(groups):
            cols = slice(g * HEAD_DIM, (g + 1) * HEAD_DIM)
            stats[k, g].wait_recv()
            packed = jnp.concatenate([stat_in[k, g], pad], axis=0).T
            scores = inner[k, g]
            top = jnp.where(
                continues, lanes_to_heads(packed[:rows], ratio, 0), jnp.max(scores, axis=1, keepdims=True)
            )
            outer_total = jnp.where(continues, lanes_to_heads(packed[rows:], ratio, 0), 0.0)
            step = jnp.where(continues, lanes_to_heads(packed[:rows], ratio, ratio) * (1.0 / LEVELS), 0.0)
            weights = jnp.exp2(scores - top)
            total = jnp.sum(weights, axis=1, keepdims=True) + outer_total
            part = jnp.dot(
                weights.astype(jnp.bfloat16), bv_ref[block_of[k], :, cols], preferred_element_type=jnp.float32
            )
            sums[k, g].wait_recv()
            part = part + sum_in[k, g].astype(jnp.int32).astype(jnp.float32) * step
            result = jnp.where(live, part / total, 0.0).astype(out_ref.dtype)
            for h in range(ratio):
                at = (g * ratio + h) * HEAD_DIM
                mixed[k, :, at : at + HEAD_DIM] = result[h * rows : (h + 1) * rows, :]

    for c in range(hops):
        out_ref[c] = mixed[route_ref[0, c]]

    for k in order:
        tops[k].wait_send()
        for g in range(groups):
            asks[k, g].wait_send()
            sums[k, g].wait_send()
            stats[k, g].wait_send()


def per_device(
    queries,
    block_keys,
    block_values,
    cache_keys,
    cache_values,
    block_len,
    prefix_len,
    deferred,
    route,
):
    peers = lax.axis_size("req")
    distances = (1, peers // 4, peers // 2)
    hops, rows, width = queries.shape
    cache_rows = cache_keys.shape[1]
    groups = block_keys.shape[2] // HEAD_DIM
    ratio = width // HEAD_DIM // groups
    stacked = ratio * rows
    smem = pl.BlockSpec(memory_space=pltpu.SMEM)
    vmem = pl.BlockSpec(memory_space=pltpu.VMEM)
    hbm = pl.BlockSpec(memory_space=pl.ANY)
    keys = rows + cache_rows
    return pl.pallas_call(
        functools.partial(kernel, distances, ratio),
        out_shape=jax.ShapeDtypeStruct(queries.shape, jnp.bfloat16),
        in_specs=[smem] * 4 + [vmem] * 3 + [hbm] * 2,
        out_specs=vmem,
        scratch_shapes=[
            pltpu.VMEM(cache_keys.shape, jnp.bfloat16),
            pltpu.VMEM(cache_values.shape, jnp.bfloat16),
            pltpu.VMEM((hops, groups, stacked, HEAD_DIM), jnp.bfloat16),
            pltpu.VMEM((hops, groups, stacked, HEAD_DIM), jnp.bfloat16),
            pltpu.VMEM((hops, groups * ratio, LANES), jnp.float32),
            pltpu.VMEM((hops, groups * ratio, LANES), jnp.float32),
            pltpu.VMEM((hops, groups, stacked, HEAD_DIM), jnp.int16),
            pltpu.VMEM((hops, groups, stacked, HEAD_DIM), jnp.int16),
            pltpu.VMEM((hops, groups, 2 * ratio, LANES), jnp.float32),
            pltpu.VMEM((hops, groups, 2 * ratio, LANES), jnp.float32),
            pltpu.VMEM((hops, groups, stacked, rows), jnp.float32),
            pltpu.VMEM((hops, rows, width), jnp.bfloat16),
            pltpu.SemaphoreType.DMA((hops, 2)),
            pltpu.SemaphoreType.DMA((2, hops, groups)),
            pltpu.SemaphoreType.DMA((2, hops)),
            pltpu.SemaphoreType.DMA((2, hops, groups)),
            pltpu.SemaphoreType.DMA((2, hops, groups)),
        ],
        compiler_params=pltpu.CompilerParams(
            collective_id=0, has_side_effects=True, vmem_limit_bytes=48 * 1024 * 1024
        ),
        cost_estimate=pl.CostEstimate(
            flops=4 * hops * rows * width * keys,
            bytes_accessed=4 * queries.size + 4 * cache_keys.size,
            transcendentals=hops * rows * width // HEAD_DIM * keys,
        ),
    )(route, block_len, prefix_len, deferred, queries, block_keys, block_values, cache_keys, cache_values)


def solution(mesh):
    return jax.shard_map(
        per_device,
        mesh=mesh,
        in_specs=(
            P(("parts", "req"), None, "tensor"),
            P(("parts", "req"), None, "tensor"),
            P(("parts", "req"), None, "tensor"),
            P(("parts", "req"), None, "tensor"),
            P(("parts", "req"), None, "tensor"),
            P(("parts", "req"), None),
            P(("parts", "req"), None),
            P(("parts", "req"), None),
            P(("parts", "req"), None),
        ),
        out_specs=P(("parts", "req"), None, "tensor"),
        check_vma=False,
    )
```

time: 117 us -> 59.1 us (0.51)
  waiting for transfers between devices: 60.2 us -> 0 us
  Pallas kernels: 0 us -> 48.7 us
  other arithmetic: 14.3 us -> 0 us
  starting transfers between devices: 9.9 us -> 0 us
  local copies, waits for them, and re-layouts: 18.7 us -> 9.23 us
  between operations: 6.06 us -> 0.02 us
  matrix products: 5.76 us -> 0 us
    ppermute x9 -> x0, waiting for transfers between devices: 60.2 us -> none  [from_behind(): lax.ppermute(value, axis, [(i, (i + by) % peers) for i in range(peers)])]
    pallas_call x0 -> x1, Pallas kernels: none -> 48.7 us  [per_device(): pl.pallas_call(functools.partial(kernel, distances, ratio), out_shape=jax...]
    ppermute x9 -> x0, starting transfers between devices: 9.9 us -> none  [from_behind(): lax.ppermute(value, axis, [(i, (i + by) % peers) for i in range(peers)])]
    dot_general x6 -> x0, matrix products: 5.76 us -> none  [the longest x3 3.48 us: attend_local(): jnp.einsum('igrd,jgd->grij', query_four, keys_all, preferred_element_type...]
    sub x3 -> x0, other arithmetic: 5.51 us -> none  [attend_local(): weights = jnp.where(visible, jnp.exp(scores - highest), jnp.float32(0.0))]
    slice x7 -> x0, local copies, waits for them, and re-layouts: 4.34 us -> none  [the longest x1 1.53 us: per_device(): cache_keys[offset_index]]
    concatenate x21 -> x0, local copies, waits for them, and re-layouts: 3.72 us -> none  [the longest x9 2.09 us: attend_local(): jnp.concatenate([cache_value, block_value], axis=0)]
    concatenate x3 -> x0, other arithmetic: 2.65 us -> none  [attend_local(): visible = jnp.concatenate([outer, inner], axis=1)]
  transfers between devices with their start and end apart: 9 -> 0, of which waited for: 4 -> 0; matrix products, arithmetic and copies ran while one was open for 17% -> 0% of each run, Pallas kernels for 0% -> 0%
where the time goes in v1:
time: 59.1 us; the launch traced here: 58 us
  Pallas kernels  48.7 us (82%)
  local copies, waits for them, and re-layouts  9.23 us (16%)
    pallas_call x1, Pallas kernels, per_device(): pl.pallas_call(functools.partial(kernel, distances, ratio), out_shape=jax...  48.7 us
    unnamed x19, local copies, waits for them, and re-layouts  9.23 us

profile of v1, /device:TPU:29, one launch (start us, length us, event | category | flops | bytes accessed | tf_op | source)
XLA Modules:
  0.0 58.0 jit_solution(9307129883636997287)
XLA Ops:
  0.0 0.0 copy-start
  0.0 1.4 %copy-done = bf16[3,1024,256]{2,1,0:T(8,128)(2,1)S(1)} copy-done((bf16[3,1024,256]{2,1,0:T(8,128)(2,1)S(1)}, bf16[3,1024,256]{2,1,0:T(8,128)(2,1)}, u32[]{:S(2)}) %copy-start) | copy-done | bytes 1572888
  1.4 0.0 copy-start.1
  1.4 1.4 %copy-done.1 = bf16[3,1024,256]{2,1,0:T(8,128)(2,1)S(1)} copy-done((bf16[3,1024,256]{2,1,0:T(8,128)(2,1)S(1)}, bf16[3,1024,256]{2,1,0:T(8,128)(2,1)}, u32[]{:S(2)}) %copy-start.1) | copy-done | bytes 1572888
  2.8 0.0 copy-start.2
  2.8 1.1 %copy-done.2 = bf16[3,64,2048]{2,1,0:T(8,128)(2,1)S(1)} copy-done((bf16[3,64,2048]{2,1,0:T(8,128)(2,1)S(1)}, bf16[3,64,2048]{2,1,0:T(8,128)(2,1)}, u32[]{:S(2)}) %copy-start.2) | copy-done | bytes 786456
  4.0 0.0 copy-start.3
  4.0 0.9 %copy-done.3 = bf16[3,64,256]{2,1,0:T(8,128)(2,1)S(1)} copy-done((bf16[3,64,256]{2,1,0:T(8,128)(2,1)S(1)}, bf16[3,64,256]{2,1,0:T(8,128)(2,1)}, u32[]{:S(2)}) %copy-start.3) | copy-done | bytes 98328
  4.8 0.0 copy-start.4
  4.8 0.9 %copy-done.4 = bf16[3,64,256]{2,1,0:T(8,128)(2,1)S(1)} copy-done((bf16[3,64,256]{2,1,0:T(8,128)(2,1)S(1)}, bf16[3,64,256]{2,1,0:T(8,128)(2,1)}, u32[]{:S(2)}) %copy-start.4) | copy-done | bytes 98328
  5.7 0.0 copy-start.5
  5.7 0.7 %copy-done.5 = s32[1,3]{1,0:T(1,128)S(1)} copy-done((s32[1,3]{1,0:T(1,128)S(1)}, s32[1,3]{1,0:T(1,128)}, u32[]{:S(2)}) %copy-start.5) | copy-done | bytes 36
  6.4 0.0 copy-start.6
  6.4 0.7 %copy-done.6 = s32[1,3]{1,0:T(1,128)S(1)} copy-done((s32[1,3]{1,0:T(1,128)S(1)}, s32[1,3]{1,0:T(1,128)}, u32[]{:S(2)}) %copy-start.6) | copy-done | bytes 36
  7.0 0.0 copy-start.7
  7.1 0.7 %copy-done.7 = s32[1,3]{1,0:T(1,128)S(1)} copy-done((s32[1,3]{1,0:T(1,128)S(1)}, s32[1,3]{1,0:T(1,128)}, u32[]{:S(2)}) %copy-start.7) | copy-done | bytes 36
  7.7 0.0 copy-start.8
  7.7 0.7 %copy-done.8 = s32[1,3]{1,0:T(1,128)S(1)} copy-done((s32[1,3]{1,0:T(1,128)S(1)}, s32[1,3]{1,0:T(1,128)}, u32[]{:S(2)}) %copy-start.8) | copy-done | bytes 36
  8.4 48.7 %shard_map.91 = bf16[3,64,2048]{2,1,0:T(8,128)(2,1)S(1)} custom-call(s32[1,3]{1,0:T(1,128)S(1)} %copy-done.5, s32[1,3]{1,0:T(1,128)S(1)} %copy-done.6, s32[1,3]{1,0:T(1,128)S(1)} %copy-done.7, s32[1,3]{1,0:T(1,128)S(1)} %copy-done.8, bf16[3,64,2048]{2,1,0:T(8,128)(2,1)S(1)} %copy-done.2, bf16[3,64,256]{2,1,0:T(8,128)(2,1)S(1)} %copy-done.3, ...), custom_call_target="tpu_custom_call" | custom-call | flops 1711276032 | bytes 4718592 | tf_op jit(solution)/shard_map/pallas_call | solution.py:231
  57.1 0.9 %copy.11 = bf16[3,64,2048]{2,1,0:T(8,128)(2,1)} copy(bf16[3,64,2048]{2,1,0:T(8,128)(2,1)S(1)} %shard_map.91) | data formatting | bytes 1572864
Async XLA Ops:
  0.0 1.4 %copy-start = (bf16[3,1024,256]{2,1,0:T(8,128)(2,1)S(1)}, bf16[3,1024,256]{2,1,0:T(8,128)(2,1)}, u32[]{:S(2)}) copy-start(bf16[3,1024,256]{2,1,0:T(8,128)(2,1)} %ck_hbm.1) | copy-start | bytes 4718596
  1.4 1.4 %copy-start.1 = (bf16[3,1024,256]{2,1,0:T(8,128)(2,1)S(1)}, bf16[3,1024,256]{2,1,0:T(8,128)(2,1)}, u32[]{:S(2)}) copy-start(bf16[3,1024,256]{2,1,0:T(8,128)(2,1)} %cv_hbm.1) | copy-start | bytes 4718596
  2.8 1.1 %copy-start.2 = (bf16[3,64,2048]{2,1,0:T(8,128)(2,1)S(1)}, bf16[3,64,2048]{2,1,0:T(8,128)(2,1)}, u32[]{:S(2)}) copy-start(bf16[3,64,2048]{2,1,0:T(8,128)(2,1)} %q_ref.1) | copy-start | bytes 2359300
  4.0 0.9 %copy-start.3 = (bf16[3,64,256]{2,1,0:T(8,128)(2,1)S(1)}, bf16[3,64,256]{2,1,0:T(8,128)(2,1)}, u32[]{:S(2)}) copy-start(bf16[3,64,256]{2,1,0:T(8,128)(2,1)} %bk_ref.1) | copy-start | bytes 294916
  4.8 0.9 %copy-start.4 = (bf16[3,64,256]{2,1,0:T(8,128)(2,1)S(1)}, bf16[3,64,256]{2,1,0:T(8,128)(2,1)}, u32[]{:S(2)}) copy-start(bf16[3,64,256]{2,1,0:T(8,128)(2,1)} %bv_ref.1) | copy-start | bytes 294916
  5.7 0.7 %copy-start.5 = (s32[1,3]{1,0:T(1,128)S(1)}, s32[1,3]{1,0:T(1,128)}, u32[]{:S(2)}) copy-start(s32[1,3]{1,0:T(1,128)} %route_ref.1) | copy-start | bytes 40
  6.4 0.7 %copy-start.6 = (s32[1,3]{1,0:T(1,128)S(1)}, s32[1,3]{1,0:T(1,128)}, u32[]{:S(2)}) copy-start(s32[1,3]{1,0:T(1,128)} %block_len_ref.1) | copy-start | bytes 40
  7.0 0.7 %copy-start.7 = (s32[1,3]{1,0:T(1,128)S(1)}, s32[1,3]{1,0:T(1,128)}, u32[]{:S(2)}) copy-start(s32[1,3]{1,0:T(1,128)} %prefix_len_ref.1) | copy-start | bytes 40
  7.7 0.7 %copy-start.8 = (s32[1,3]{1,0:T(1,128)S(1)}, s32[1,3]{1,0:T(1,128)}, u32[]{:S(2)}) copy-start(s32[1,3]{1,0:T(1,128)} %deferred_ref.1) | copy-start | bytes 40

commit v2 on v1

--- a/solution.py
+++ b/solution.py
@@ -35,6 +35,16 @@
 def kernel(
     distances,
     ratio,
+    route_hbm,
+    block_len_hbm,
+    prefix_len_hbm,
+    deferred_hbm,
+    q_hbm,
+    bk_hbm,
+    bv_hbm,
+    ck_hbm,
+    cv_hbm,
+    out_hbm,
     route_ref,
     block_len_ref,
     prefix_len_ref,
@@ -42,9 +52,6 @@
     q_ref,
     bk_ref,
     bv_ref,
-    ck_hbm,
-    cv_hbm,
-    out_ref,
     ck,
     cv,
     q_out,
@@ -57,7 +64,9 @@
     stat_in,
     inner,
     mixed,
+    small_sem,
     cache_sem,
+    out_sem,
     q_sem,
     top_sem,
     sum_sem,
@@ -70,6 +79,7 @@
     cache_rows = ck.shape[1]
     stacked = ratio * rows
     order = list(reversed(range(hops)))
+    steps = [(k, g) for g in range(groups) for k in order]
     holder = [lax.rem(me + distances[k], peers) for k in range(hops)]
     asker = [lax.rem(me + peers - distances[k], peers) for k in range(hops)]
 
@@ -78,6 +88,22 @@
         for peer in (holder[k], asker[k]):
             pl.semaphore_signal(barrier, inc=1, device_id={"req": peer}, device_id_type=MESH)
 
+    small = [
+        pltpu.make_async_copy(source, target, small_sem.at[i])
+        for i, (source, target) in enumerate(
+            [
+                (q_hbm, q_ref),
+                (route_hbm, route_ref),
+                (block_len_hbm, block_len_ref),
+                (bk_hbm, bk_ref),
+                (prefix_len_hbm, prefix_len_ref),
+                (deferred_hbm, deferred_ref),
+                (bv_hbm, bv_ref),
+            ]
+        )
+    ]
+    for load in small:
+        load.start()
     loads = {}
     for k in order:
         loads[k] = [
@@ -87,6 +113,8 @@
         for load in loads[k]:
             load.start()
 
+    for load in small[:2]:
+        load.wait()
     block_of = []
     for k in range(hops):
         block = jnp.int32(0)
@@ -104,19 +132,17 @@
             device_id_type=MESH,
         )
 
-    for k in order:
-        for g in range(groups):
-            for h in range(ratio):
-                at = (g * ratio + h) * HEAD_DIM
-                q_out[k, g, h * rows : (h + 1) * rows, :] = q_ref[block_of[k], :, at : at + HEAD_DIM]
-
-    pl.semaphore_wait(barrier, 2 * hops)
-
     asks, tops, sums, stats = {}, {}, {}, {}
-    for k in order:
-        for g in range(groups):
-            asks[k, g] = send(q_out, q_in, q_sem, (k, g), holder[k])
-            asks[k, g].start()
+    for k, g in steps:
+        for h in range(ratio):
+            at = (g * ratio + h) * HEAD_DIM
+            q_out[k, g, h * rows : (h + 1) * rows, :] = q_ref[block_of[k], :, at : at + HEAD_DIM]
+        if (k, g) == steps[0]:
+            pl.semaphore_wait(barrier, 2 * hops)
+        asks[k, g] = send(q_out, q_in, q_sem, (k, g), holder[k])
+        asks[k, g].start()
+    for load in small[2:]:
+        load.wait()
 
     row = lax.rem(lax.broadcasted_iota(jnp.int32, (stacked, rows), 0), rows)
     column = lax.broadcasted_iota(jnp.int32, (stacked, rows), 1)
@@ -138,65 +164,67 @@
 
     place = lax.broadcasted_iota(jnp.int32, (1, cache_rows), 1)
     pad = jnp.zeros((LANES - groups * ratio, LANES), jnp.float32)
-    for k in order:
+    for k, g in steps:
         bias = jnp.where(place < prefix_len_ref[0, k], 0.0, HIDDEN)
-        for load in loads[k]:
-            load.wait()
-        tops[k].wait_recv()
+        if k in loads:
+            for load in loads.pop(k):
+                load.wait()
+            tops[k].wait_recv()
         asked_top = jnp.concatenate([top_in[k], pad], axis=0).T[:rows, :]
-        for g in range(groups):
-            cols = slice(g * HEAD_DIM, (g + 1) * HEAD_DIM)
-            asks[k, g].wait_recv()
-            scores = dot_nt(q_in[k, g], ck[k, :, cols]) * SCALE + bias
-            top = jnp.maximum(
-                lanes_to_heads(asked_top, ratio, g * ratio), jnp.max(scores, axis=1, keepdims=True)
-            )
-            weights = jnp.exp2(scores - top)
-            total = jnp.sum(weights, axis=1, keepdims=True)
-            part = jnp.dot(
-                weights.astype(jnp.bfloat16), cv[k, :, cols], preferred_element_type=jnp.float32
-            )
-            largest = jnp.maximum(jnp.max(jnp.abs(part), axis=1, keepdims=True), 1e-33)
-            coded = jnp.round(part * (LEVELS / largest))
-            sum_out[k, g] = coded.astype(jnp.int32).astype(jnp.int16)
-            sums[k, g] = send(sum_out, sum_in, sum_sem, (k, g), asker[k])
-            sums[k, g].start()
-            zeros = jnp.zeros((rows, LANES), jnp.float32)
-            upper = heads_to_lanes(top, rows, ratio, 0, zeros)
-            upper = heads_to_lanes(largest, rows, ratio, ratio, upper)
-            lower = heads_to_lanes(total, rows, ratio, 0, zeros)
-            stat_out[k, g] = jnp.concatenate([upper, lower], axis=0).T[: 2 * ratio, :]
-            stats[k, g] = send(stat_out, stat_in, stat_sem, (k, g), asker[k])
-            stats[k, g].start()
+        cols = slice(g * HEAD_DIM, (g + 1) * HEAD_DIM)
+        asks[k, g].wait_recv()
+        scores = dot_nt(q_in[k, g], ck[k, :, cols]) * SCALE + bias
+        top = jnp.maximum(
+            lanes_to_heads(asked_top, ratio, g * ratio), jnp.max(scores, axis=1, keepdims=True)
+        )
+        weights = jnp.exp2(scores - top)
+        total = jnp.sum(weights, axis=1, keepdims=True)
+        part = jnp.dot(
+            weights.astype(jnp.bfloat16), cv[k, :, cols], preferred_element_type=jnp.float32
+        )
+        largest = jnp.maximum(jnp.max(jnp.abs(part), axis=1, keepdims=True), 1e-33)
+        coded = jnp.round(part * (LEVELS / largest))
+        sum_out[k, g] = coded.astype(jnp.int32).astype(jnp.int16)
+        sums[k, g] = send(sum_out, sum_in, sum_sem, (k, g), asker[k])
+        sums[k, g].start()
+        zeros = jnp.zeros((rows, LANES), jnp.float32)
+        upper = heads_to_lanes(top, rows, ratio, 0, zeros)
+        upper = heads_to_lanes(largest, rows, ratio, ratio, upper)
+        lower = heads_to_lanes(total, rows, ratio, 0, zeros)
+        stat_out[k, g] = jnp.concatenate([upper, lower], axis=0).T[: 2 * ratio, :]
+        stats[k, g] = send(stat_out, stat_in, stat_sem, (k, g), asker[k])
+        stats[k, g].start()
 
     pad = jnp.zeros((LANES - 2 * ratio, LANES), jnp.float32)
-    for k in order:
+    for k, g in steps:
         continues = deferred_ref[0, block_of[k]] == 1
         live = row[:, :1] < block_len_ref[0, block_of[k]]
-        for g in range(groups):
-            cols = slice(g * HEAD_DIM, (g + 1) * HEAD_DIM)
-            stats[k, g].wait_recv()
-            packed = jnp.concatenate([stat_in[k, g], pad], axis=0).T
-            scores = inner[k, g]
-            top = jnp.where(
-                continues, lanes_to_heads(packed[:rows], ratio, 0), jnp.max(scores, axis=1, keepdims=True)
-            )
-            outer_total = jnp.where(continues, lanes_to_heads(packed[rows:], ratio, 0), 0.0)
-            step = jnp.where(continues, lanes_to_heads(packed[:rows], ratio, ratio) * (1.0 / LEVELS), 0.0)
-            weights = jnp.exp2(scores - top)
-            total = jnp.sum(weights, axis=1, keepdims=True) + outer_total
-            part = jnp.dot(
-                weights.astype(jnp.bfloat16), bv_ref[block_of[k], :, cols], preferred_element_type=jnp.float32
-            )
-            sums[k, g].wait_recv()
-            part = part + sum_in[k, g].astype(jnp.int32).astype(jnp.float32) * step
-            result = jnp.where(live, part / total, 0.0).astype(out_ref.dtype)
-            for h in range(ratio):
-                at = (g * ratio + h) * HEAD_DIM
-                mixed[k, :, at : at + HEAD_DIM] = result[h * rows : (h + 1) * rows, :]
-
+        cols = slice(g * HEAD_DIM, (g + 1) * HEAD_DIM)
+        stats[k, g].wait_recv()
+        packed = jnp.concatenate([stat_in[k, g], pad], axis=0).T
+        scores = inner[k, g]
+        top = jnp.where(
+            continues, lanes_to_heads(packed[:rows], ratio, 0), jnp.max(scores, axis=1, keepdims=True)
+        )
+        outer_total = jnp.where(continues, lanes_to_heads(packed[rows:], ratio, 0), 0.0)
+        step = jnp.where(continues, lanes_to_heads(packed[:rows], ratio, ratio) * (1.0 / LEVELS), 0.0)
+        weights = jnp.exp2(scores - top)
+        total = jnp.sum(weights, axis=1, keepdims=True) + outer_total
+        part = jnp.dot(
+            weights.astype(jnp.bfloat16), bv_ref[block_of[k], :, cols], preferred_element_type=jnp.float32
+        )
+        sums[k, g].wait_recv()
+        part = part + sum_in[k, g].astype(jnp.int32).astype(jnp.float32) * step
+        result = jnp.where(live, part / total, 0.0).astype(mixed.dtype)
+        for h in range(ratio):
+            at = (g * ratio + h) * HEAD_DIM
+            mixed[k, :, at : at + HEAD_DIM] = result[h * rows : (h + 1) * rows, :]
+
+    stores = []
     for c in range(hops):
-        out_ref[c] = mixed[route_ref[0, c]]
+        q_ref[c] = mixed[route_ref[0, c]]
+        stores.append(pltpu.make_async_copy(q_ref.at[c], out_hbm.at[c], out_sem.at[c]))
+        stores[c].start()
 
     for k in order:
         tops[k].wait_send()
@@ -204,6 +232,8 @@
             asks[k, g].wait_send()
             sums[k, g].wait_send()
             stats[k, g].wait_send()
+    for store in stores:
+        store.wait()
 
 
 def per_device(
@@ -224,16 +254,21 @@
     groups = block_keys.shape[2] // HEAD_DIM
     ratio = width // HEAD_DIM // groups
     stacked = ratio * rows
-    smem = pl.BlockSpec(memory_space=pltpu.SMEM)
-    vmem = pl.BlockSpec(memory_space=pltpu.VMEM)
-    hbm = pl.BlockSpec(memory_space=pl.ANY)
+    hbm = pl.BlockSpec(memory_space=pltpu.HBM)
     keys = rows + cache_rows
     return pl.pallas_call(
         functools.partial(kernel, distances, ratio),
         out_shape=jax.ShapeDtypeStruct(queries.shape, jnp.bfloat16),
-        in_specs=[smem] * 4 + [vmem] * 3 + [hbm] * 2,
-        out_specs=vmem,
+        in_specs=[hbm] * 9,
+        out_specs=hbm,
         scratch_shapes=[
+            pltpu.SMEM(route.shape, jnp.int32),
+            pltpu.SMEM(block_len.shape, jnp.int32),
+            pltpu.SMEM(prefix_len.shape, jnp.int32),
+            pltpu.SMEM(deferred.shape, jnp.int32),
+            pltpu.VMEM(queries.shape, jnp.bfloat16),
+            pltpu.VMEM(block_keys.shape, jnp.bfloat16),
+            pltpu.VMEM(block_values.shape, jnp.bfloat16),
             pltpu.VMEM(cache_keys.shape, jnp.bfloat16),
             pltpu.VMEM(cache_values.shape, jnp.bfloat16),
             pltpu.VMEM((hops, groups, stacked, HEAD_DIM), jnp.bfloat16),
@@ -246,14 +281,16 @@
             pltpu.VMEM((hops, groups, 2 * ratio, LANES), jnp.float32),
             pltpu.VMEM((hops, groups, stacked, rows), jnp.float32),
             pltpu.VMEM((hops, rows, width), jnp.bfloat16),
+            pltpu.SemaphoreType.DMA((7,)),
             pltpu.SemaphoreType.DMA((hops, 2)),
+            pltpu.SemaphoreType.DMA((hops,)),
             pltpu.SemaphoreType.DMA((2, hops, groups)),
             pltpu.SemaphoreType.DMA((2, hops)),
             pltpu.SemaphoreType.DMA((2, hops, groups)),
             pltpu.SemaphoreType.DMA((2, hops, groups)),
         ],
         compiler_params=pltpu.CompilerParams(
-            collective_id=0, has_side_effects=True, vmem_limit_bytes=48 * 1024 * 1024
+            collective_id=0, has_side_effects=True, vmem_limit_bytes=64 * 1024 * 1024 - 65536
         ),
         cost_estimate=pl.CostEstimate(
             flops=4 * hops * rows * width * keys,

time: 59.1 us -> 51.2 us (0.87); the launches traced: 58 us -> 51.1 us
  local copies, waits for them, and re-layouts: 9.23 us -> 2.09 us
    unnamed x19 -> x1, local copies, waits for them, and re-layouts: 9.23 us -> 2.09 us
where the time goes in v2:
time: 51.2 us; the launch traced here: 51.1 us
  Pallas kernels  49 us (96%)
  local copies, waits for them, and re-layouts  2.09 us (4%)
    pallas_call x1, Pallas kernels, per_device(): pl.pallas_call(functools.partial(kernel, distances, ratio), out_shape=jax...  49 us
    unnamed x1, local copies, waits for them, and re-layouts  2.09 us

profile of v2, /device:TPU:29, one launch (start us, length us, event | category | flops | bytes accessed | tf_op | source)
XLA Modules:
  0.0 51.1 jit_solution(6348993056460171500)
XLA Ops:
  0.0 49.0 %shard_map.91 = bf16[3,64,2048]{2,1,0:T(8,128)(2,1)} custom-call(s32[1,3]{1,0:T(1,128)} %route_hbm.1, s32[1,3]{1,0:T(1,128)} %block_len_hbm.1, s32[1,3]{1,0:T(1,128)} %prefix_len_hbm.1, s32[1,3]{1,0:T(1,128)} %deferred_hbm.1, bf16[3,64,2048]{2,1,0:T(8,128)(2,1)} %q_hbm.1, bf16[3,64,256]{2,1,0:T(8,128)(2,1)} %bk_hbm.1, bf16[3,64,256]{2,1,0:T(8,128)(2,1)} %bv_hbm.1, ...), custom_call_target="tpu_custom_call" | custom-call | flops 1711276032 | bytes 4718592 | tf_op jit(solution)/shard_map/pallas_call | solution.py:259
  49.0 2.1 %copy.11 = bf16[3,64,2048]{2,1,0:T(8,128)(2,1)} copy(bf16[3,64,2048]{2,1,0:T(8,128)(2,1)} %shard_map.91) | data formatting | bytes 1572864

commit v3 on v2

--- a/solution.py
+++ b/solution.py
@@ -185,8 +185,6 @@
         largest = jnp.maximum(jnp.max(jnp.abs(part), axis=1, keepdims=True), 1e-33)
         coded = jnp.round(part * (LEVELS / largest))
         sum_out[k, g] = coded.astype(jnp.int32).astype(jnp.int16)
-        sums[k, g] = send(sum_out, sum_in, sum_sem, (k, g), asker[k])
-        sums[k, g].start()
         zeros = jnp.zeros((rows, LANES), jnp.float32)
         upper = heads_to_lanes(top, rows, ratio, 0, zeros)
         upper = heads_to_lanes(largest, rows, ratio, ratio, upper)
@@ -194,6 +192,8 @@
         stat_out[k, g] = jnp.concatenate([upper, lower], axis=0).T[: 2 * ratio, :]
         stats[k, g] = send(stat_out, stat_in, stat_sem, (k, g), asker[k])
         stats[k, g].start()
+        sums[k, g] = send(sum_out, sum_in, sum_sem, (k, g), asker[k])
+        sums[k, g].start()
 
     pad = jnp.zeros((LANES - 2 * ratio, LANES), jnp.float32)
     for k, g in steps:

time: 51.2 us -> 50.7 us (level)
  no operation moved by 1% of the time
where the time goes in v3:
time: 50.7 us; the launch traced here: 50.6 us
  Pallas kernels  48.5 us (96%)
  local copies, waits for them, and re-layouts  2.09 us (4%)
    pallas_call x1, Pallas kernels, per_device(): pl.pallas_call(functools.partial(kernel, distances, ratio), out_shape=jax...  48.5 us
    unnamed x1, local copies, waits for them, and re-layouts  2.09 us

profile of v3, /device:TPU:29, one launch (start us, length us, event | category | flops | bytes accessed | tf_op | source)
XLA Modules:
  0.0 50.6 jit_solution(10130946035868134954)
XLA Ops:
  0.0 48.5 %shard_map.91 = bf16[3,64,2048]{2,1,0:T(8,128)(2,1)} custom-call(s32[1,3]{1,0:T(1,128)} %route_hbm.1, s32[1,3]{1,0:T(1,128)} %block_len_hbm.1, s32[1,3]{1,0:T(1,128)} %prefix_len_hbm.1, s32[1,3]{1,0:T(1,128)} %deferred_hbm.1, bf16[3,64,2048]{2,1,0:T(8,128)(2,1)} %q_hbm.1, bf16[3,64,256]{2,1,0:T(8,128)(2,1)} %bk_hbm.1, bf16[3,64,256]{2,1,0:T(8,128)(2,1)} %bv_hbm.1, ...), custom_call_target="tpu_custom_call" | custom-call | flops 1711276032 | bytes 4718592 | tf_op jit(solution)/shard_map/pallas_call | solution.py:259
  48.5 2.1 %copy.11 = bf16[3,64,2048]{2,1,0:T(8,128)(2,1)} copy(bf16[3,64,2048]{2,1,0:T(8,128)(2,1)} %shard_map.91) | data formatting | bytes 1572864
